TPU v7x, 512 devices: a whole 4x4x16 slice. The times are simulated.
512 devices in a mesh: tm: 8 (over z_hi, core), tile: 16 (over x, y), head: 4 (over z_lo).
Axes of the slice: x: 4, y: 4, z: 16 (z_hi: 4, z_lo: 4; z = z_hi * 4 + z_lo), core: 2. Of those that a mesh axis runs over, the one named last changes fastest.
Arguments:
- query: bfloat16 [8, 16, 2, 16, 16, 1536], P('tm', 'tile', None, None, None, 'head'), may hold values from -80 to 80
- keys: bfloat16 [8, 16, 2, 16, 16, 1536], P('tm', 'tile', None, None, None, 'head'), may hold values from -80 to 80
- values: bfloat16 [8, 16, 2, 16, 16, 1536], P('tm', 'tile', None, None, None, 'head'), may hold values from -6 to 6
- out_weight: bfloat16 [1536, 1536], P('head'), may hold values from -0.15625 to 0.15625
- radius: int32 [12], P('head'), may hold values from 1 to 4
- block_mask: int32 [12, 8, 8], P('head'), may hold values from 0 to 1, as said below
Outputs:
- mixed: bfloat16 [8, 16, 512, 1536], P('tm', 'tile', 'head')
Inputs may be any that keep to these rules, and one draw needn't show every extreme that they name: For every head, block_mask is 1 on the diagonal of its table and 0 above it.
All inputs are finite; a program needn't handle non-finite values.
Results may differ from a plain program's by a relative error of at most 0.015.
Values may be sent and summed in bfloat16 or wider, within the bound.
A program may use at most 128 MiB of HBM per device.

v0:
```python
import math
import jax
import jax.numpy as jnp
from jax import lax
from jax.sharding import PartitionSpec as P

RMAX = 4


def passed_along(value, axis, by):
    peers = lax.axis_size(axis)
    pairs = [(i, i + by) for i in range(peers) if 0 <= i + by < peers]
    return lax.ppermute(value, axis, pairs)


def widen(key_part, value_part, span, row_move, col_move):
    grid = math.isqrt(lax.axis_size("tile"))
    above = None
    below = None
    for offset in (grid, -grid):
        if offset > 0:
            face_key = key_part[:, :, key_part.shape[2] - span :]
            face_value = value_part[:, :, value_part.shape[2] - span :]
        else:
            face_key = key_part[:, :, :span]
            face_value = value_part[:, :, :span]
        got = row_move(face_key, face_value, offset)
        if offset > 0:
            above = got
        else:
            below = got
    key_rows = jnp.concatenate([above[0], key_part, below[0]], axis=2)
    value_rows = jnp.concatenate([above[1], value_part, below[1]], axis=2)
    left = None
    right = None
    for offset in (1, -1):
        if offset > 0:
            face_key = key_rows[:, :, :, key_rows.shape[3] - span :]
            face_value = value_rows[:, :, :, value_rows.shape[3] - span :]
        else:
            face_key = key_rows[:, :, :, :span]
            face_value = value_rows[:, :, :, :span]
        got = col_move(face_key, face_value, offset)
        if offset > 0:
            left = got
        else:
            right = got
    key_full = jnp.concatenate([left[0], key_rows, right[0]], axis=3)
    value_full = jnp.concatenate([left[1], value_rows, right[1]], axis=3)
    return (key_full, value_full)


def windows_of(block, half_high, half_wide, win_high, win_wide, heads_here, head_dim):
    parts = []
    for band in (0, 1):
        for strip in (0, 1):
            parts.append(
                block[
                    :,
                    band * half_high : band * half_high + win_high,
                    strip * half_wide : strip * half_wide + win_wide,
                ]
            )
    stacked = jnp.stack(parts)
    return stacked.reshape(4, -1, heads_here, head_dim)


def per_device(query, keys, values, out_weight, radius, block_mask):
    span = RMAX
    grid = math.isqrt(lax.axis_size("tile"))
    tile_at = lax.axis_index("tile")
    row_at = tile_at // grid
    col_at = tile_at % grid
    stretch_at = lax.axis_index("tm")
    frames, high, wide, channels = query.shape[2:]
    heads_here = radius.shape[0]
    head_dim = channels // heads_here
    tokens_here = frames * high * wide
    half_high = high // 2
    half_wide = wide // 2
    win_high = half_high + 2 * span
    win_wide = half_wide + 2 * span
    quarter = frames * half_high * half_wide
    queries = query[0, 0].reshape(frames, 2, half_high, 2, half_wide, channels)
    queries = queries.transpose(1, 3, 0, 2, 4, 5).reshape(4, quarter, heads_here, head_dim)
    query_y = jnp.broadcast_to(
        jnp.arange(half_high, dtype=jnp.int32)[None, :, None], (frames, half_high, half_wide)
    ).reshape(-1)
    query_x = jnp.broadcast_to(
        jnp.arange(half_wide, dtype=jnp.int32)[None, None, :], (frames, half_high, half_wide)
    ).reshape(-1)
    key_y = jnp.broadcast_to(
        jnp.arange(win_high, dtype=jnp.int32)[None, :, None] - span, (frames, win_high, win_wide)
    ).reshape(-1)
    key_x = jnp.broadcast_to(
        jnp.arange(win_wide, dtype=jnp.int32)[None, None, :] - span, (frames, win_high, win_wide)
    ).reshape(-1)
    band_at = jnp.array([0, 0, 1, 1], dtype=jnp.int32)
    strip_at = jnp.array([0, 1, 0, 1], dtype=jnp.int32)
    global_y = row_at * high + band_at[:, None] * half_high + key_y[None, :]
    global_x = col_at * wide + strip_at[:, None] * half_wide + key_x[None, :]
    inside = (global_y >= 0) & (global_y < grid * high) & (global_x >= 0) & (global_x < grid * wide)
    distance = jnp.maximum(
        jnp.abs(query_y[:, None] - key_y[None, :]), jnp.abs(query_x[:, None] - key_x[None, :])
    )
    near = distance[None, :, :] <= radius[:, None, None]
    allowed = near[None, :, :, :] & inside[:, None, None, :]
    scale = 1.0 / math.sqrt(head_dim)
    initial = (
        jnp.full((4, heads_here, quarter), -1e30, jnp.float32),
        jnp.zeros((4, heads_here, quarter), jnp.float32),
        jnp.zeros((4, heads_here, quarter, head_dim), jnp.float32),
    )

    def all_row_move(face_key, face_value, offset):
        return passed_along((face_key, face_value), "tile", offset)

    def all_col_move(face_key, face_value, offset):
        return passed_along((face_key, face_value), "tile", offset)

    key_all, value_all = (
        lax.all_gather(keys[0], "tm", axis=0, tiled=True),
        lax.all_gather(values[0], "tm", axis=0, tiled=True),
    )
    key_full, value_full = widen(key_all, value_all, span, all_row_move, all_col_move)
    piece = (key_full, value_full)
    count = piece[0].shape[0]
    stretch_ids = jnp.arange(count, dtype=jnp.int32)

    def one_stretch(state, item):
        key_block, value_block, stretch_id = item
        visible = (
            lax.dynamic_slice_in_dim(
                lax.dynamic_index_in_dim(block_mask, stretch_at, 1, False), stretch_id, 1, 1
            )[:, 0]
            > 0
        )
        best, total, acc = state
        key_win = windows_of(
            key_block, half_high, half_wide, win_high, win_wide, heads_here, head_dim
        )
        value_win = windows_of(
            value_block, half_high, half_wide, win_high, win_wide, heads_here, head_dim
        )
        usable = allowed & visible[None, :, None, None]
        scores = (
            jnp.einsum("nqhd,nkhd->nhqk", queries, key_win, preferred_element_type=jnp.float32)
            * scale
        )
        masked = jnp.where(usable, scores, jnp.float32(-1e30))
        fresh = jnp.maximum(best, jnp.max(masked, axis=3))
        probs = jnp.where(usable, jnp.exp(scores - fresh[..., None]), jnp.float32(0.0))
        shrink = jnp.exp(best - fresh)
        total = total * shrink + jnp.sum(probs, axis=3)
        acc = acc * shrink[..., None] + jnp.einsum(
            "nhqk,nkhd->nhqd",
            probs.astype(jnp.bfloat16),
            value_win,
            preferred_element_type=jnp.float32,
        )
        result = (fresh, total, acc)
        return (result, None)

    final, unused = lax.scan(one_stretch, initial, (piece[0], piece[1], stretch_ids))
    best, total, acc = final
    attn = (acc / total[..., None]).astype(jnp.bfloat16)
    attn = attn.transpose(0, 2, 1, 3).reshape(
        2, 2, frames, half_high, half_wide, heads_here * head_dim
    )
    attn = attn.transpose(2, 0, 3, 1, 4, 5).reshape(tokens_here, heads_here * head_dim)
    mixed = lax.psum_scatter(
        jnp.dot(attn, out_weight, preferred_element_type=jnp.float32).astype(jnp.bfloat16),
        "head",
        scatter_dimension=0,
        tiled=True,
    )
    return mixed.reshape(1, 1, -1, out_weight.shape[1])


def solution(mesh):
    in_specs = (
        P("tm", "tile", None, None, None, "head"),
        P("tm", "tile", None, None, None, "head"),
        P("tm", "tile", None, None, None, "head"),
        P("head", None),
        P("head"),
        P("head", None, None),
    )
    out_specs = P("tm", "tile", "head", None)
    return jax.shard_map(
        per_device, mesh=mesh, in_specs=in_specs, out_specs=out_specs, check_vma=False
    )
```

profile of v0, /device:TPU:1, one launch (start us, length us, event | category | flops | bytes accessed | tf_op | source)
XLA Modules:
  0.0 517.4 jit_solution(15858110646869679896)
XLA Ops:
  8.1 85.1 %all-gather.7.cloned.1.call-done = bf16[8,1,2,16,16,384]{5,4,3,2,1,0:T(8,128)(2,1)} async-done(((bf16[1,1,2,16,16,384]{5,4,3,2,1,0:T(8,128)(2,1)}), bf16[8,1,2,16,16,384]{5,4,3,2,1,0:T(8,128)(2,1)}) %all-gather.7.cloned.1.call-update) | async-done | bytes 3145744 | tf_op jit(solution)/shard_map/all_gather | solution.py:123
  93.2 2.5 fusion.46
  95.7 3.8 collective-permute-start.4
  102.1 14.4 %collective-permute-done.4 = bf16[8,2,4,16,384]{4,3,2,1,0:T(8,128)(2,1)S(1)} collective-permute-done((bf16[8,2,4,16,384]{4,3,2,1,0:T(8,128)(2,1)}, bf16[8,2,4,16,384]{4,3,2,1,0:T(8,128)(2,1)S(1)}, u32[]{:S(2)}, u32[]{:S(2)}) %collective-permute-start.4) | collective-permute-done | bytes 786464 | tf_op jit(solution)/shard_map/ppermute | solution.py:13
  116.5 3.6 collective-permute-done.5
  120.1 3.5 pad_maximum_fusion.4
  123.6 4.2 collective-permute-start.6
  129.0 40.4 %all-gather.5.cloned.1.call-done = bf16[8,1,2,16,16,384]{5,4,3,2,1,0:T(8,128)(2,1)} async-done(((bf16[1,1,2,16,16,384]{5,4,3,2,1,0:T(8,128)(2,1)}), bf16[8,1,2,16,16,384]{5,4,3,2,1,0:T(8,128)(2,1)}) %all-gather.5.cloned.1.call-update) | async-done | bytes 3145744 | tf_op jit(solution)/shard_map/all_gather | solution.py:122
  169.5 2.8 fusion.47
  172.2 3.8 collective-permute-start
  186.3 1.8 copy.45
  188.1 2.1 reshape.220
  190.2 1.9 copy.40
  192.0 1.4 copy.39
  195.7 1.5 broadcast_compare_fusion
  197.2 2.9 pad_maximum_fusion.7
  200.1 3.2 collective-permute-start.2
  203.3 1.7 collective-permute-start.3
  205.1 7.7 %pad_maximum_fusion.1 = bf16[8,2,24,24,384]{4,3,2,1,0:T(8,128)(2,1)} fusion(bf16[8,2,24,4,384]{4,3,2,1,0:T(4,128)(2,1)} %collective-permute-done.7, bf16[8,2,4,16,384]{4,3,2,1,0:T(8,128)(2,1)S(1)} %collective-permute-done.5, bf16[8,2,16,16,384]{4,3,2,1,0:T(8,128)(2,1)S(1)} %bitcast.74, bf16[8,2,4,16,384]{4,3,2,1,0:T(8,128)(2,1)S(1)} %collective-permute-done.4, ...), kind=kLoop, calls=%fused_computation.46 | loop fusion | flops 35389440 | bytes 14155776 | tf_op jit(solution)/shard_map/concatenate | solution.py:49
  212.8 14.5 %collective-permute-done.2 = bf16[8,2,24,4,384]{4,3,2,1,0:T(4,128)(2,1)S(1)} collective-permute-done((bf16[8,2,24,4,384]{4,3,2,1,0:T(4,128)(2,1)S(1)}, bf16[8,2,24,4,384]{4,3,2,1,0:T(4,128)(2,1)S(1)}, u32[]{:S(2)}, u32[]{:S(2)}) %collective-permute-start.2) | collective-permute-done | bytes 1179680 | tf_op jit(solution)/shard_map/ppermute | solution.py:13
  227.4 4.2 collective-permute-done.3
  231.5 7.6 %pad_maximum_fusion = bf16[8,2,24,24,384]{4,3,2,1,0:T(8,128)(2,1)} fusion(bf16[8,2,24,4,384]{4,3,2,1,0:T(4,128)(2,1)S(1)} %collective-permute-done.3, bf16[8,2,4,16,384]{4,3,2,1,0:T(8,128)(2,1)} %collective-permute-done.1, bf16[8,2,16,16,384]{4,3,2,1,0:T(8,128)(2,1)S(1)} %bitcast.71, bf16[8,2,4,16,384]{4,3,2,1,0:T(8,128)(2,1)S(1)} %collective-permute-done, ...), kind=kLoop, calls=%fused_computation.45 | loop fusion | flops 35389440 | bytes 14155776 | tf_op jit(solution)/shard_map/concatenate | solution.py:48
  239.1 221.7 %while.18 = (s32[]{:T(128)}, f32[4,3,128]{2,1,0:T(4,128)S(1)}, f32[4,3,128]{2,1,0:T(4,128)S(1)}, f32[4,3,128,128]{3,2,1,0:T(8,128)}, s32[8]{0:T(128)S(1)}, /*ind...) while((s32[]{:T(128)}, f32[4,3,128]{2,1,0:T(4,128)S(1)}, ...), condition=%wide.region_3.4_spmd.clone, body=%wide.region_0.3_spmd.clone.sunk | while | flops 421338624 | bytes 41597296 | solution.py:164
  242.2 1.6 dynamic-slice_bitcast_fusion.3
  244.9 1.4 stack.48
  250.4 4.0 fusion.64
  254.4 2.4 fusion.65
  262.2 4.4 fusion.68
  269.7 1.6 dynamic-slice_bitcast_fusion.3
  272.4 1.4 stack.48
  277.9 4.0 fusion.64
  281.9 2.4 fusion.65
  289.7 4.7 fusion.68
  297.5 1.6 dynamic-slice_bitcast_fusion.3
  300.1 1.4 stack.48
  305.7 4.0 fusion.64
  309.7 2.4 fusion.65
  317.4 4.7 fusion.68
  325.2 1.6 dynamic-slice_bitcast_fusion.3
  327.9 1.4 stack.48
  333.4 4.0 fusion.64
  337.4 2.4 fusion.65
  345.2 4.7 fusion.68
  353.0 1.6 dynamic-slice_bitcast_fusion.3
  361.2 4.0 fusion.64
  365.2 2.4 fusion.65
  372.9 4.7 fusion.68
  380.7 1.6 dynamic-slice_bitcast_fusion.3
  383.4 1.4 stack.48
  388.9 4.0 fusion.64
  392.9 2.4 fusion.65
  400.7 4.7 fusion.68
  408.5 1.6 dynamic-slice_bitcast_fusion.3
  411.1 1.4 stack.48
  416.6 4.0 fusion.64
  420.7 2.4 fusion.65
  428.4 4.7 fusion.68
  436.2 1.6 dynamic-slice_bitcast_fusion.3
  444.4 4.0 fusion.64
  448.4 2.4 fusion.65
  456.1 4.7 fusion.68
  460.8 1.4 fusion.40
  463.0 2.2 convolution_convert_fusion
  465.2 45.7 %reduce-scatter.2.cloned.1.call-done = bf16[128,1536]{1,0:T(8,128)(2,1)} async-done(((bf16[512,1536]{1,0:T(8,128)(2,1)}), bf16[128,1536]{1,0:T(8,128)(2,1)}) %reduce-scatter.2.cloned.1.call-update) | async-done | bytes 393232 | tf_op jit(solution)/shard_map/reduce_scatter | solution.py:171
  (282 shorter events, 114.4 us)
Async XLA Ops:
  6.5 456.4 %copy-start = (bf16[384,1536]{1,0:T(8,128)(2,1)S(1)}, bf16[384,1536]{1,0:T(8,128)(2,1)}, u32[]{:S(2)}) copy-start(bf16[384,1536]{1,0:T(8,128)(2,1)} %param.13) | copy-start | bytes 3538948
  6.5 86.7 %all-gather.7.cloned.1.call-start = ((), (), s32[]{:S(2)}) async-start(), calls=%async_computation.3 | async-start | bytes 3538944 | tf_op jit(solution)/shard_map/all_gather | solution.py:123
  7.3 162.2 %all-gather.5.cloned.1.call-start = ((), (), s32[]{:S(2)}) async-start(), calls=%async_computation.2 | async-start | bytes 3538944 | tf_op jit(solution)/shard_map/all_gather | solution.py:122
  8.0 502.9 %reduce-scatter.2.cloned.1.call-start = ((), (), s32[]{:S(2)}) async-start(), calls=%async_computation.1 | async-start | bytes 1966080 | tf_op jit(solution)/shard_map/reduce_scatter | solution.py:171
  95.7 20.8 %collective-permute-start.4 = (bf16[8,2,4,16,384]{4,3,2,1,0:T(8,128)(2,1)}, bf16[8,2,4,16,384]{4,3,2,1,0:T(8,128)(2,1)S(1)}, u32[]{:S(2)}, u32[]{:S(2)}) collective-permute-start(bf16[8,2,4,16,384]{4,3,2,1,0:T(8,128)(2,1)} %get-tuple-element.310), channel_id=1, source_target_pairs={{0,16},{4,20},{8,24},{12,28},{16,32},{20,36},{24,40},{28,44},{32,4... | collective-permute-start | bytes 2359304 | tf_op jit(solution)/shard_map/ppermute | solution.py:13
  99.5 20.6 %collective-permute-start.5 = (bf16[8,2,4,16,384]{4,3,2,1,0:T(8,128)(2,1)S(1)}, bf16[8,2,4,16,384]{4,3,2,1,0:T(8,128)(2,1)S(1)}, u32[]{:S(2)}, u32[]{:S(2)}) collective-permute-start(bf16[8,2,4,16,384]{4,3,2,1,0:T(8,128)(2,1)S(1)} %get-tuple-element.311), channel_id=1, source_target_pairs={{16,0},{20,4},{24,8},{28,12},{32,16},{36,20},{40,24},{44,28},{48,3... | collective-permute-start | bytes 2359304 | tf_op jit(solution)/shard_map/ppermute | solution.py:13
  123.6 81.5 %collective-permute-start.6 = (bf16[8,2,24,4,384]{4,3,2,1,0:T(4,128)(2,1)}, bf16[8,2,24,4,384]{4,3,2,1,0:T(4,128)(2,1)}, u32[]{:S(2)}, u32[]{:S(2)}) collective-permute-start(bf16[8,2,24,4,384]{4,3,2,1,0:T(4,128)(2,1)} %get-tuple-element.306), channel_id=1, source_target_pairs={{0,4},{4,8},{8,12},{12,16},{16,20},{20,24},{24,28},{28,32},{32,36}... | collective-permute-start | bytes 3538952 | tf_op jit(solution)/shard_map/ppermute | solution.py:13
  127.8 77.3 %collective-permute-start.7 = (bf16[8,2,24,4,384]{4,3,2,1,0:T(4,128)(2,1)}, bf16[8,2,24,4,384]{4,3,2,1,0:T(4,128)(2,1)}, u32[]{:S(2)}, u32[]{:S(2)}) collective-permute-start(bf16[8,2,24,4,384]{4,3,2,1,0:T(4,128)(2,1)} %get-tuple-element.307), channel_id=1, source_target_pairs={{4,0},{8,4},{12,8},{16,12},{20,16},{24,20},{28,24},{32,28},{36,32}... | collective-permute-start | bytes 3538952 | tf_op jit(solution)/shard_map/ppermute | solution.py:13
  172.2 24.9 %collective-permute-start = (bf16[8,2,4,16,384]{4,3,2,1,0:T(8,128)(2,1)}, bf16[8,2,4,16,384]{4,3,2,1,0:T(8,128)(2,1)S(1)}, u32[]{:S(2)}, u32[]{:S(2)}) collective-permute-start(bf16[8,2,4,16,384]{4,3,2,1,0:T(8,128)(2,1)} %get-tuple-element.312), channel_id=1, source_target_pairs={{0,16},{4,20},{8,24},{12,28},{16,32},{20,36},{24,40},{28,44},{32,4... | collective-permute-start | bytes 2359304 | tf_op jit(solution)/shard_map/ppermute | solution.py:13
  176.1 21.1 %collective-permute-start.1 = (bf16[8,2,4,16,384]{4,3,2,1,0:T(8,128)(2,1)}, bf16[8,2,4,16,384]{4,3,2,1,0:T(8,128)(2,1)}, u32[]{:S(2)}, u32[]{:S(2)}) collective-permute-start(bf16[8,2,4,16,384]{4,3,2,1,0:T(8,128)(2,1)} %get-tuple-element.313), channel_id=1, source_target_pairs={{16,0},{20,4},{24,8},{28,12},{32,16},{36,20},{40,24},{44,28},{48,3... | collective-permute-start | bytes 2359304 | tf_op jit(solution)/shard_map/ppermute | solution.py:13
  177.4 0.5 copy-start.7
  197.2 7.9 %copy-start.2 = (bf16[8,1,2,16,16,384]{5,4,3,2,1,0:T(8,128)(2,1)S(1)}, bf16[8,1,2,16,16,384]{5,4,3,2,1,0:T(8,128)(2,1)}, u32[]{:S(2)}) copy-start(bf16[8,1,2,16,16,384]{5,4,3,2,1,0:T(8,128)(2,1)} %all-gather.7.cloned.1.call-done) | copy-start | bytes 9437188
  200.1 27.2 %collective-permute-start.2 = (bf16[8,2,24,4,384]{4,3,2,1,0:T(4,128)(2,1)S(1)}, bf16[8,2,24,4,384]{4,3,2,1,0:T(4,128)(2,1)S(1)}, u32[]{:S(2)}, u32[]{:S(2)}) collective-permute-start(bf16[8,2,24,4,384]{4,3,2,1,0:T(4,128)(2,1)S(1)} %get-tuple-element.308), channel_id=1, source_target_pairs={{0,4},{4,8},{8,12},{12,16},{16,20},{20,24},{24,28},{28,32},{32,36}... | collective-permute-start | bytes 3538952 | tf_op jit(solution)/shard_map/ppermute | solution.py:13
  203.3 28.2 %copy-start.1 = (bf16[8,1,2,16,16,384]{5,4,3,2,1,0:T(8,128)(2,1)S(1)}, bf16[8,1,2,16,16,384]{5,4,3,2,1,0:T(8,128)(2,1)}, u32[]{:S(2)}) copy-start(bf16[8,1,2,16,16,384]{5,4,3,2,1,0:T(8,128)(2,1)} %all-gather.5.cloned.1.call-done) | copy-start | bytes 9437188
  203.3 28.2 %collective-permute-start.3 = (bf16[8,2,24,4,384]{4,3,2,1,0:T(4,128)(2,1)S(1)}, bf16[8,2,24,4,384]{4,3,2,1,0:T(4,128)(2,1)S(1)}, u32[]{:S(2)}, u32[]{:S(2)}) collective-permute-start(bf16[8,2,24,4,384]{4,3,2,1,0:T(4,128)(2,1)S(1)} %get-tuple-element.309), channel_id=1, source_target_pairs={{4,0},{8,4},{12,8},{16,12},{20,16},{24,20},{28,24},{32,28},{36,32}... | collective-permute-start | bytes 3538952 | tf_op jit(solution)/shard_map/ppermute | solution.py:13
  248.5 1.9 copy-start.6
  250.4 4.0 copy-start.5
  260.1 1.9 copy-start.3
  261.1 1.1 copy-start.4
  276.0 1.9 copy-start.6
  277.9 4.0 copy-start.5
  287.6 1.9 copy-start.3
  288.6 1.1 copy-start.4
  303.7 1.9 copy-start.6
  305.7 4.0 copy-start.5
  315.4 1.9 copy-start.3
  316.3 1.1 copy-start.4
  331.5 1.9 copy-start.6
  333.4 4.0 copy-start.5
  343.1 1.9 copy-start.3
  344.1 1.1 copy-start.4
  359.2 1.9 copy-start.6
  361.1 4.0 copy-start.5
  370.9 1.9 copy-start.3
  371.8 1.1 copy-start.4
  387.0 1.9 copy-start.6
  388.9 4.0 copy-start.5
  398.6 1.9 copy-start.3
  399.6 1.1 copy-start.4
  414.7 1.9 copy-start.6
  416.6 4.0 copy-start.5
  426.4 1.9 copy-start.3
  427.3 1.1 copy-start.4
  442.5 1.9 copy-start.6
  444.4 4.0 copy-start.5
  454.1 1.9 copy-start.3
  455.1 1.1 copy-start.4
Sparse Core Ops, SparseCore 0:
  9.5 83.6 all-gather.6
  95.3 74.1 all-gather.4
  465.3 45.5 reduce-scatter.1
where the time goes:
time: 520 us; the launch traced here: 517 us
  waiting for transfers between devices  209 us (40%)
  local copies, waits for them, and re-layouts  134 us (26%)
  matrix products  71.3 us (14%)
  other arithmetic  53.4 us (10%)
  starting transfers between devices  20.7 us (4%)
  loops' own time  15.8 us (3%)
  between operations  13.3 us (3%)
    all_gather x1, waiting for transfers between devices, per_device(): lax.all_gather(values[0], 'tm', axis=0, tiled=True)  85.1 us
    another operation x128, local copies, waits for them, and re-layouts, windows_of(): stacked = jnp.stack(parts)  77.2 us
    reduce_scatter x1, waiting for transfers between devices, per_device(): lax.psum_scatter(jnp.dot(attn, out_weight, preferred_element_type=jnp.flo...  45.7 us
    all_gather x1, waiting for transfers between devices, per_device(): lax.all_gather(keys[0], 'tm', axis=0, tiled=True)  40.4 us
    dot_general x8, matrix products, one_stretch(): jnp.einsum('nhqk,nkhd->nhqd', probs.astype(jnp.bfloat16), value_win, pref...  37.1 us
    ppermute x8, waiting for transfers between devices, passed_along(): return lax.ppermute(value, axis, pairs)  36.7 us
    dot_general x8, matrix products, one_stretch(): jnp.einsum('nqhd,nkhd->nhqk', queries, key_win, preferred_element_type=jn...  32 us
    ppermute x8, starting transfers between devices, passed_along(): return lax.ppermute(value, axis, pairs)  20.6 us
  transfers between devices with their start and end apart: 11, of which 7 were waited for; matrix products, arithmetic and copies ran while one was open for 8% of the time, Pallas kernels for 0%

commit v1 on v0

--- a/solution.py
+++ b/solution.py
@@ -120,7 +120,15 @@
 
     key_all, value_all = (
         lax.all_gather(keys[0], "tm", axis=0, tiled=True),
-        lax.all_gather(values[0], "tm", axis=0, tiled=True),
+        jnp.concatenate(
+            lax.all_to_all(
+                jnp.stack([values[0]] * lax.axis_size("tm")),
+                axis_name="tm",
+                split_axis=0,
+                concat_axis=0,
+            ),
+            axis=0,
+        ),
     )
     key_full, value_full = widen(key_all, value_all, span, all_row_move, all_col_move)
     piece = (key_full, value_full)

time: 520 us -> 621 us (1.19)
  waiting for transfers between devices: 209 us -> 292 us
  starting transfers between devices: 20.7 us -> 35.7 us
    all_gather x1, waiting for transfers between devices: 40.4 us -> 197 us  [per_device(): lax.all_gather(keys[0], 'tm', axis=0, tiled=True)]
    all_gather x1 -> x0, waiting for transfers between devices: 85.1 us -> none  [per_device(): lax.all_gather(values[0], 'tm', axis=0, tiled=True)]
    all_to_all x0 -> x1, starting transfers between devices: none -> 16.6 us  [per_device(): lax.all_to_all(jnp.stack([values[0]] * lax.axis_size('tm')), axis_name='t...]
    ppermute x8, waiting for transfers between devices: 36.7 us -> 50.7 us  [passed_along(): return lax.ppermute(value, axis, pairs)]
  transfers between devices with their start and end apart: 11 -> 11, of which waited for: 7 -> 7; matrix products, arithmetic and copies ran while one was open for 8% -> 6% of each run, Pallas kernels for 0% -> 0%
where the time goes in v1:
time: 621 us; the launch traced here: 618 us
  waiting for transfers between devices  292 us (47%)
  local copies, waits for them, and re-layouts  137 us (22%)
  matrix products  71.3 us (11%)
  other arithmetic  54.2 us (9%)
  starting transfers between devices  35.7 us (6%)
  loops' own time  14.3 us (2%)
  between operations  13.6 us (2%)
    all_gather x1, waiting for transfers between devices, per_device(): lax.all_gather(keys[0], 'tm', axis=0, tiled=True)  197 us
    another operation x128, local copies, waits for them, and re-layouts, windows_of(): stacked = jnp.stack(parts)  77.3 us
    ppermute x8, waiting for transfers between devices, passed_along(): return lax.ppermute(value, axis, pairs)  50.7 us
    reduce_scatter x1, waiting for transfers between devices, per_device(): lax.psum_scatter(jnp.dot(attn, out_weight, preferred_element_type=jnp.flo...  44 us
    dot_general x8, matrix products, one_stretch(): jnp.einsum('nhqk,nkhd->nhqd', probs.astype(jnp.bfloat16), value_win, pref...  37.1 us
    dot_general x8, matrix products, one_stretch(): jnp.einsum('nqhd,nkhd->nhqk', queries, key_win, preferred_element_type=jn...  32 us
    reduce_sum x8, other arithmetic, one_stretch(): total = total * shrink + jnp.sum(probs, axis=3)  19.6 us
    ppermute x8, starting transfers between devices, passed_along(): return lax.ppermute(value, axis, pairs)  19.1 us
  transfers between devices with their start and end apart: 11, of which 7 were waited for; matrix products, arithmetic and copies ran while one was open for 6% of the time, Pallas kernels for 0%

profile of v1, /device:TPU:1, one launch (start us, length us, event | category | flops | bytes accessed | tf_op | source)
XLA Modules:
  0.0 618.0 jit_solution(15428805428925460804)
XLA Ops:
  6.5 3.2 stack.33
  9.7 16.6 %all-to-all-start = ((bf16[8,1,2,16,16,384]{5,4,3,2,1,0:T(8,128)(2,1)}), bf16[8,1,2,16,16,384]{5,4,3,2,1,0:T(8,128)(2,1)}, u32[]{:S(2)}, u32[]{:S(2)}) async-start(bf16[8,1,2,16,16,384]{5,4,3,2,1,0:T(8,128)(2,1)} %stack.33), calls=%async_computation | async-start | bytes 6291456 | tf_op jit(solution)/shard_map/all_to_all | solution.py:124
  27.1 196.8 %all-gather.3.cloned.1.call-done = bf16[8,1,2,16,16,384]{5,4,3,2,1,0:T(8,128)(2,1)} async-done(((bf16[1,1,2,16,16,384]{5,4,3,2,1,0:T(8,128)(2,1)}), bf16[8,1,2,16,16,384]{5,4,3,2,1,0:T(8,128)(2,1)}) %all-gather.3.cloned.1.call-update) | async-done | bytes 3145744 | tf_op jit(solution)/shard_map/all_gather | solution.py:122
  223.9 2.5 fusion.47
  226.4 3.2 collective-permute-start
  232.1 14.3 %collective-permute-done = bf16[8,2,4,16,384]{4,3,2,1,0:T(8,128)(2,1)S(1)} collective-permute-done((bf16[8,2,4,16,384]{4,3,2,1,0:T(8,128)(2,1)}, bf16[8,2,4,16,384]{4,3,2,1,0:T(8,128)(2,1)S(1)}, u32[]{:S(2)}, u32[]{:S(2)}) %collective-permute-start) | collective-permute-done | bytes 786464 | tf_op jit(solution)/shard_map/ppermute | solution.py:13
  246.4 3.5 collective-permute-done.1
  250.0 3.5 pad_maximum_fusion.7
  253.5 4.3 collective-permute-start.2
  259.1 2.8 fusion.46
  261.9 4.9 collective-permute-start.4
  272.1 1.4 sub.89
  277.3 1.8 copy.43
  279.0 2.0 reshape.226
  281.1 1.9 copy.38
  283.0 1.4 copy.37
  286.6 1.5 broadcast_compare_fusion
  288.1 15.4 %collective-permute-done.5 = bf16[8,2,4,16,384]{4,3,2,1,0:T(8,128)(2,1)} collective-permute-done((bf16[8,2,4,16,384]{4,3,2,1,0:T(8,128)(2,1)}, bf16[8,2,4,16,384]{4,3,2,1,0:T(8,128)(2,1)}, u32[]{:S(2)}, u32[]{:S(2)}) %collective-permute-start.5) | collective-permute-done | bytes 786464 | tf_op jit(solution)/shard_map/ppermute | solution.py:13
  303.5 2.8 pad_maximum_fusion.4
  307.7 1.5 collective-permute-start.7
  309.2 7.7 %pad_maximum_fusion = bf16[8,2,24,24,384]{4,3,2,1,0:T(8,128)(2,1)} fusion(bf16[8,2,24,4,384]{4,3,2,1,0:T(4,128)(2,1)} %collective-permute-done.3, bf16[8,2,4,16,384]{4,3,2,1,0:T(8,128)(2,1)S(1)} %collective-permute-done.1, bf16[8,2,16,16,384]{4,3,2,1,0:T(8,128)(2,1)S(1)} %bitcast.72, bf16[8,2,4,16,384]{4,3,2,1,0:T(8,128)(2,1)S(1)} %collective-permute-done, ...), kind=kLoop, calls=%fused_computation.45 | loop fusion | flops 35389440 | bytes 14155776 | tf_op jit(solution)/shard_map/concatenate | solution.py:48
  316.9 13.6 %collective-permute-done.6 = bf16[8,2,24,4,384]{4,3,2,1,0:T(4,128)(2,1)S(1)} collective-permute-done((bf16[8,2,24,4,384]{4,3,2,1,0:T(4,128)(2,1)S(1)}, bf16[8,2,24,4,384]{4,3,2,1,0:T(4,128)(2,1)S(1)}, u32[]{:S(2)}, u32[]{:S(2)}) %collective-permute-start.6) | collective-permute-done | bytes 1179680 | tf_op jit(solution)/shard_map/ppermute | solution.py:13
  330.5 3.9 collective-permute-done.7
  334.4 8.4 %pad_maximum_fusion.1 = bf16[8,2,24,24,384]{4,3,2,1,0:T(8,128)(2,1)} fusion(bf16[8,2,24,4,384]{4,3,2,1,0:T(4,128)(2,1)S(1)} %collective-permute-done.7, bf16[8,2,4,16,384]{4,3,2,1,0:T(8,128)(2,1)} %collective-permute-done.5, bf16[8,2,16,16,384]{4,3,2,1,0:T(8,128)(2,1)} %bitcast.4, bf16[8,2,4,16,384]{4,3,2,1,0:T(8,128)(2,1)S(1)} %collective-permute-done.4, ...), kind=kLoop, calls=%fused_computation.46 | loop fusion | flops 35389440 | bytes 14155776 | tf_op jit(solution)/shard_map/concatenate | solution.py:49
  342.8 220.0 %while.18 = (s32[]{:T(128)}, f32[4,3,128]{2,1,0:T(4,128)S(1)}, f32[4,3,128]{2,1,0:T(4,128)S(1)}, f32[4,3,128,128]{3,2,1,0:T(8,128)}, s32[8]{0:T(128)S(1)}, /*ind...) while((s32[]{:T(128)}, f32[4,3,128]{2,1,0:T(4,128)S(1)}, ...), condition=%wide.region_3.4_spmd.clone, body=%wide.region_0.3_spmd.clone.sunk | while | flops 421338624 | bytes 41597296 | solution.py:172
  345.7 1.6 dynamic-slice_bitcast_fusion.3
  353.9 4.0 fusion.64
  358.0 2.4 fusion.65
  365.7 4.4 fusion.68
  373.0 1.6 dynamic-slice_bitcast_fusion.3
  375.7 1.4 stack.52
  381.2 4.0 fusion.64
  385.2 2.4 fusion.65
  393.0 4.7 fusion.68
  400.5 1.6 dynamic-slice_bitcast_fusion.3
  403.2 1.4 stack.52
  408.7 4.0 fusion.64
  412.8 2.4 fusion.65
  420.5 4.7 fusion.68
  428.1 1.6 dynamic-slice_bitcast_fusion.3
  430.7 1.4 stack.52
  436.3 4.0 fusion.64
  440.3 2.4 fusion.65
  448.0 4.7 fusion.68
  455.6 1.6 dynamic-slice_bitcast_fusion.3
  458.3 1.4 stack.52
  463.8 4.0 fusion.64
  467.8 2.4 fusion.65
  475.6 4.7 fusion.68
  483.1 1.6 dynamic-slice_bitcast_fusion.3
  491.3 4.0 fusion.64
  495.4 2.4 fusion.65
  503.1 4.7 fusion.68
  510.7 1.6 dynamic-slice_bitcast_fusion.3
  518.9 4.0 fusion.64
  522.9 2.4 fusion.65
  530.6 4.7 fusion.68
  538.2 1.6 dynamic-slice_bitcast_fusion.3
  546.4 4.0 fusion.64
  550.4 2.4 fusion.65
  558.2 4.7 fusion.68
  562.8 1.4 fusion.40
  565.0 2.2 convolution_convert_fusion
  567.2 44.0 %reduce-scatter.2.cloned.1.call-done = bf16[128,1536]{1,0:T(8,128)(2,1)} async-done(((bf16[512,1536]{1,0:T(8,128)(2,1)}), bf16[128,1536]{1,0:T(8,128)(2,1)}) %reduce-scatter.2.cloned.1.call-update) | async-done | bytes 393232 | tf_op jit(solution)/shard_map/reduce_scatter | solution.py:179
  (280 shorter events, 116.4 us)
Async XLA Ops:
  6.5 558.5 %copy-start = (bf16[384,1536]{1,0:T(8,128)(2,1)S(1)}, bf16[384,1536]{1,0:T(8,128)(2,1)}, u32[]{:S(2)}) copy-start(bf16[384,1536]{1,0:T(8,128)(2,1)} %param.13) | copy-start | bytes 3538948
  9.7 249.4 %all-to-all-start = ((bf16[8,1,2,16,16,384]{5,4,3,2,1,0:T(8,128)(2,1)}), bf16[8,1,2,16,16,384]{5,4,3,2,1,0:T(8,128)(2,1)}, u32[]{:S(2)}, u32[]{:S(2)}) async-start(bf16[8,1,2,16,16,384]{5,4,3,2,1,0:T(8,128)(2,1)} %stack.33), calls=%async_computation | async-start | bytes 6291456 | tf_op jit(solution)/shard_map/all_to_all | solution.py:124
  26.3 197.6 %all-gather.3.cloned.1.call-start = ((), (), s32[]{:S(2)}) async-start(), calls=%async_computation.3 | async-start | bytes 3538944 | tf_op jit(solution)/shard_map/all_gather | solution.py:122
  27.0 584.2 %reduce-scatter.2.cloned.1.call-start = ((), (), s32[]{:S(2)}) async-start(), calls=%async_computation.2 | async-start | bytes 1966080 | tf_op jit(solution)/shard_map/reduce_scatter | solution.py:179
  226.4 20.1 %collective-permute-start = (bf16[8,2,4,16,384]{4,3,2,1,0:T(8,128)(2,1)}, bf16[8,2,4,16,384]{4,3,2,1,0:T(8,128)(2,1)S(1)}, u32[]{:S(2)}, u32[]{:S(2)}) collective-permute-start(bf16[8,2,4,16,384]{4,3,2,1,0:T(8,128)(2,1)} %get-tuple-element.312), channel_id=1, source_target_pairs={{0,16},{4,20},{8,24},{12,28},{16,32},{20,36},{24,40},{28,44},{32,4... | collective-permute-start | bytes 2359304 | tf_op jit(solution)/shard_map/ppermute | solution.py:13
  229.5 20.4 %collective-permute-start.1 = (bf16[8,2,4,16,384]{4,3,2,1,0:T(8,128)(2,1)S(1)}, bf16[8,2,4,16,384]{4,3,2,1,0:T(8,128)(2,1)S(1)}, u32[]{:S(2)}, u32[]{:S(2)}) collective-permute-start(bf16[8,2,4,16,384]{4,3,2,1,0:T(8,128)(2,1)S(1)} %get-tuple-element.313), channel_id=1, source_target_pairs={{16,0},{20,4},{24,8},{28,12},{32,16},{36,20},{40,24},{44,28},{48,3... | collective-permute-start | bytes 2359304 | tf_op jit(solution)/shard_map/ppermute | solution.py:13
  253.5 55.7 %collective-permute-start.2 = (bf16[8,2,24,4,384]{4,3,2,1,0:T(4,128)(2,1)}, bf16[8,2,24,4,384]{4,3,2,1,0:T(4,128)(2,1)}, u32[]{:S(2)}, u32[]{:S(2)}) collective-permute-start(bf16[8,2,24,4,384]{4,3,2,1,0:T(4,128)(2,1)} %get-tuple-element.308), channel_id=1, source_target_pairs={{0,4},{4,8},{8,12},{12,16},{16,20},{20,24},{24,28},{28,32},{32,36}... | collective-permute-start | bytes 3538952 | tf_op jit(solution)/shard_map/ppermute | solution.py:13
  257.8 51.3 %collective-permute-start.3 = (bf16[8,2,24,4,384]{4,3,2,1,0:T(4,128)(2,1)}, bf16[8,2,24,4,384]{4,3,2,1,0:T(4,128)(2,1)}, u32[]{:S(2)}, u32[]{:S(2)}) collective-permute-start(bf16[8,2,24,4,384]{4,3,2,1,0:T(4,128)(2,1)} %get-tuple-element.309), channel_id=1, source_target_pairs={{4,0},{8,4},{12,8},{16,12},{20,16},{24,20},{28,24},{32,28},{36,32}... | collective-permute-start | bytes 3538952 | tf_op jit(solution)/shard_map/ppermute | solution.py:13
  261.9 26.2 %collective-permute-start.4 = (bf16[8,2,4,16,384]{4,3,2,1,0:T(8,128)(2,1)}, bf16[8,2,4,16,384]{4,3,2,1,0:T(8,128)(2,1)S(1)}, u32[]{:S(2)}, u32[]{:S(2)}) collective-permute-start(bf16[8,2,4,16,384]{4,3,2,1,0:T(8,128)(2,1)} %get-tuple-element.310), channel_id=1, source_target_pairs={{0,16},{4,20},{8,24},{12,28},{16,32},{20,36},{24,40},{28,44},{32,4... | collective-permute-start | bytes 2359304 | tf_op jit(solution)/shard_map/ppermute | solution.py:13
  266.8 36.7 %collective-permute-start.5 = (bf16[8,2,4,16,384]{4,3,2,1,0:T(8,128)(2,1)}, bf16[8,2,4,16,384]{4,3,2,1,0:T(8,128)(2,1)}, u32[]{:S(2)}, u32[]{:S(2)}) collective-permute-start(bf16[8,2,4,16,384]{4,3,2,1,0:T(8,128)(2,1)} %get-tuple-element.311), channel_id=1, source_target_pairs={{16,0},{20,4},{24,8},{28,12},{32,16},{36,20},{40,24},{44,28},{48,3... | collective-permute-start | bytes 2359304 | tf_op jit(solution)/shard_map/ppermute | solution.py:13
  268.1 0.6 copy-start.6
  288.1 21.0 %copy-start.1 = (bf16[8,1,2,16,16,384]{5,4,3,2,1,0:T(8,128)(2,1)S(1)}, bf16[8,1,2,16,16,384]{5,4,3,2,1,0:T(8,128)(2,1)}, u32[]{:S(2)}) copy-start(bf16[8,1,2,16,16,384]{5,4,3,2,1,0:T(8,128)(2,1)} %all-gather.3.cloned.1.call-done) | copy-start | bytes 9437188
  306.3 24.2 %collective-permute-start.6 = (bf16[8,2,24,4,384]{4,3,2,1,0:T(4,128)(2,1)S(1)}, bf16[8,2,24,4,384]{4,3,2,1,0:T(4,128)(2,1)S(1)}, u32[]{:S(2)}, u32[]{:S(2)}) collective-permute-start(bf16[8,2,24,4,384]{4,3,2,1,0:T(4,128)(2,1)S(1)} %get-tuple-element.306), channel_id=1, source_target_pairs={{0,4},{4,8},{8,12},{12,16},{16,20},{20,24},{24,28},{28,32},{32,36}... | collective-permute-start | bytes 3538952 | tf_op jit(solution)/shard_map/ppermute | solution.py:13
  307.7 26.7 %collective-permute-start.7 = (bf16[8,2,24,4,384]{4,3,2,1,0:T(4,128)(2,1)S(1)}, bf16[8,2,24,4,384]{4,3,2,1,0:T(4,128)(2,1)S(1)}, u32[]{:S(2)}, u32[]{:S(2)}) collective-permute-start(bf16[8,2,24,4,384]{4,3,2,1,0:T(4,128)(2,1)S(1)} %get-tuple-element.307), channel_id=1, source_target_pairs={{4,0},{8,4},{12,8},{16,12},{20,16},{24,20},{28,24},{32,28},{36,32}... | collective-permute-start | bytes 3538952 | tf_op jit(solution)/shard_map/ppermute | solution.py:13
  352.0 1.9 copy-start.5
  353.9 4.0 copy-start.4
  363.6 1.9 copy-start.2
  364.6 1.1 copy-start.3
  379.3 1.9 copy-start.5
  381.2 4.0 copy-start.4
  390.9 1.9 copy-start.2
  391.9 1.1 copy-start.3
  406.8 1.9 copy-start.5
  408.7 4.0 copy-start.4
  418.5 1.9 copy-start.2
  419.4 1.1 copy-start.3
  434.3 1.9 copy-start.5
  436.3 4.0 copy-start.4
  446.0 1.9 copy-start.2
  446.9 1.1 copy-start.3
  461.9 1.9 copy-start.5
  463.8 4.0 copy-start.4
  473.5 1.9 copy-start.2
  474.5 1.1 copy-start.3
  489.4 1.9 copy-start.5
  491.3 4.0 copy-start.4
  501.1 1.9 copy-start.2
  502.0 1.1 copy-start.3
  516.9 1.9 copy-start.5
  518.9 4.0 copy-start.4
  528.6 1.9 copy-start.2
  529.5 1.1 copy-start.3
  544.5 1.9 copy-start.5
  546.4 4.0 copy-start.4
  556.1 1.9 copy-start.2
  557.1 1.1 copy-start.3
Sparse Core Ops, SparseCore 0:
  29.2 194.5 all-gather.2
  567.3 43.8 reduce-scatter.1
